TPU v7x, 32 devices: a whole 2x2x4 slice. The times are simulated.
32 devices in a mesh: groups: 1, frames: 32 (over z, y, x, core).
Axes of the slice: x: 2, y: 2, z: 4, core: 2. Of those that a mesh axis runs over, the one named last changes fastest.
Arguments:
- skip: bfloat16 [32, 256, 640], P(('groups', 'frames')), may hold values from -24 to 24
- control: bfloat16 [32, 256, 640], P('groups', 'frames'), may hold values from -6 to 6
- zero_weight: bfloat16 [640, 640], replicated, may hold values from -1 to 1
- gn_gain: float32 [640], replicated, may hold values from 0.1 to 1.9
- gn_bias: float32 [640], replicated, may hold values from -0.5 to 0.5
- conv_weight: bfloat16 [9, 640, 640], replicated, may hold values from -0.078125 to 0.078125
- ln_gain: float32 [640], replicated, may hold values from 0.1 to 1.9
- qkv_weight: bfloat16 [640, 1920], replicated, may hold values from -5 to 5
- out_weight: bfloat16 [640, 640], replicated, may hold values from -0.25 to 0.25
Outputs:
- output: bfloat16 [32, 256, 640], P(('groups', 'frames'))
All inputs are finite; a program needn't handle non-finite values.
Results may differ from a plain program's by a relative error of at most 0.0043.
Values may be sent and summed in bfloat16 or wider, within the bound.
A program may use at most 64 MiB of HBM per device.

v0:
```python
import math

import jax
import jax.numpy as jnp
from jax import lax
from jax.sharding import PartitionSpec as P

HEADS = 10
HD = 64
GROUPS = 32
CLIP = 32
W = 32


norm_epsilon = 1e-05


def attend_block(qkv_rows, chans):
    frame_count, single, count, _ = qkv_rows.shape
    clip_count = frame_count // CLIP
    shaped = qkv_rows.reshape(clip_count, CLIP, count, 3, HEADS, HD)
    queries = shaped[:, :, :, 0]
    key_rows = shaped[:, :, :, 1]
    value_rows = shaped[:, :, :, 2]
    scores = jnp.einsum(
        "atphd,asphd->aphts", queries, key_rows, preferred_element_type=jnp.float32
    ) * (1.0 / math.sqrt(HD))
    scores = scores - jnp.max(scores, axis=-1, keepdims=True)
    expon = jnp.exp(scores)
    attn_weights = (expon / jnp.sum(expon, axis=-1, keepdims=True)).astype(jnp.bfloat16)
    mixed = jnp.einsum(
        "aphts,asphd->atphd", attn_weights, value_rows, preferred_element_type=jnp.float32
    )
    return mixed.astype(jnp.bfloat16).reshape(frame_count, single, count, chans)


def body(
    skip, control, zero_weight, gn_gain, gn_bias, conv_weight, ln_gain, qkv_weight, out_weight
):
    f_dev, pixels, chans = skip.shape
    devices = lax.axis_size("frames")
    frame_count, pix_dev, _ = control.shape
    height = pixels // W
    zero_out = jnp.dot(control.reshape(-1, chans), zero_weight, preferred_element_type=jnp.float32)
    zero_out = zero_out.astype(jnp.bfloat16).reshape(frame_count, pix_dev, chans)
    zero_frames = lax.all_to_all(zero_out, "frames", split_axis=0, concat_axis=1, tiled=True)
    joined = skip.astype(jnp.float32) + zero_frames.astype(jnp.float32)
    group_size = chans // GROUPS
    grouped = joined.reshape(f_dev, pixels, GROUPS, group_size)
    clip_count = f_dev * devices // CLIP
    frame_ids = lax.axis_index("frames") * f_dev + jnp.arange(f_dev, dtype=jnp.int32)
    member = (
        frame_ids[:, None] // CLIP == jnp.arange(clip_count, dtype=jnp.int32)[None, :]
    ).astype(jnp.float32)
    count_all = float(CLIP * pixels * group_size)
    frame_sums = jnp.sum(grouped, axis=(1, 3))
    clip_sums = jnp.sum(member[:, :, None] * frame_sums[:, None, :], axis=0)
    frame_sq = jnp.sum(jnp.square(grouped), axis=(1, 3))
    clip_sq = jnp.sum(member[:, :, None] * frame_sq[:, None, :], axis=0)
    total_sums, total_sq = lax.psum((clip_sums, clip_sq), "frames")
    clip_mean = total_sums / count_all
    clip_var = total_sq / count_all - jnp.square(clip_mean)
    frame_mean = jnp.sum(member[:, :, None] * clip_mean[None], axis=1)
    centred = grouped - frame_mean[:, None, :, None]
    frame_var = jnp.sum(member[:, :, None] * clip_var[None], axis=1)
    normed_groups = (centred * lax.rsqrt(frame_var + norm_epsilon)[:, None, :, None]).reshape(
        f_dev, pixels, chans
    )
    activated = (
        jax.nn.silu(normed_groups * gn_gain + gn_bias)
        .astype(jnp.bfloat16)
        .reshape(f_dev, height, W, chans)
    )
    padded = jnp.pad(activated, ((0, 0), (1, 1), (1, 1), (0, 0)))
    conv_sum = jnp.zeros((f_dev * pixels, chans), jnp.float32)
    for tap_index in range(9):
        row_shift, col_shift = divmod(tap_index, 3)
        window = padded[:, row_shift : row_shift + height, col_shift : col_shift + W, :].reshape(
            -1, chans
        )
        conv_sum = conv_sum + jnp.dot(
            window, conv_weight[tap_index], preferred_element_type=jnp.float32
        )
    resid = joined.reshape(-1, chans) + conv_sum
    token_mean = jnp.mean(resid, axis=-1, keepdims=True)
    token_var = jnp.mean(jnp.square(resid - token_mean), axis=-1, keepdims=True)
    normed = ((resid - token_mean) * lax.rsqrt(token_var + norm_epsilon) * ln_gain).astype(
        jnp.bfloat16
    )
    per_device = pixels // devices
    qkv_rows = jnp.dot(normed, qkv_weight, preferred_element_type=jnp.float32).astype(jnp.bfloat16)
    qkv_rows = qkv_rows.reshape(f_dev, devices, per_device, 3 * chans)
    attended = attend_block(
        lax.all_to_all(qkv_rows, "frames", split_axis=1, concat_axis=0, tiled=True), chans
    )
    returned = lax.all_to_all(attended, "frames", split_axis=0, concat_axis=1, tiled=True)
    output = resid + jnp.dot(
        returned.reshape(-1, chans), out_weight, preferred_element_type=jnp.float32
    )
    return output.astype(jnp.bfloat16).reshape(f_dev, pixels, chans)


def solution(mesh):
    in_specs = (
        P(("groups", "frames"), None, None),
        P("groups", "frames", None),
        P(),
        P(),
        P(),
        P(),
        P(),
        P(),
        P(),
    )
    out_specs = P(("groups", "frames"), None, None)
    return jax.shard_map(body, mesh=mesh, in_specs=in_specs, out_specs=out_specs, check_vma=False)
```

profile of v0, /device:TPU:0, one launch (start us, length us, event | category | flops | bytes accessed | tf_op | source)
XLA Modules:
  0.0 136.1 jit_solution(5476533162441262583)
XLA Ops:
  0.0 2.6 %fusion.7 = bf16[32,8,640]{2,1,0:T(8,128)(2,1)} fusion(bf16[640,640]{1,0:T(8,128)(2,1)} %param.11, bf16[32,8,640]{2,1,0:T(8,128)(2,1)} %param.10), kind=kOutput, calls=%fused_computation.21 | convolution fusion | flops 209879040 | bytes 1474560 | tf_op jit(solution)/shard_map/dot_general | solution.py:44
  2.6 7.3 %all-to-all-start = ((bf16[32,8,640]{2,1,0:T(8,128)(2,1)}), bf16[32,8,640]{2,1,0:T(8,128)(2,1)S(1)}, u32[]{:S(2)}, u32[]{:S(2)}) async-start(bf16[32,8,640]{2,1,0:T(8,128)(2,1)} %fusion.7), calls=%async_computation | async-start | bytes 655360 | tf_op jit(solution)/shard_map/all_to_all | solution.py:46
  9.9 12.0 %all-to-all-done = bf16[32,8,640]{2,1,0:T(8,128)(2,1)S(1)} async-done(((bf16[32,8,640]{2,1,0:T(8,128)(2,1)}), bf16[32,8,640]{2,1,0:T(8,128)(2,1)S(1)}, u32[]{:S(2)}, u32[]{:S(2)}) %all-to-all-start) | async-done | bytes 327712 | tf_op jit(solution)/shard_map/all_to_all | solution.py:46
  21.9 1.1 multiply_reduce_fusion.1
  23.4 38.6 %all-reduce.1 = (f32[1,32]{1,0:T(1,128)S(1)}, f32[1,32]{1,0:T(1,128)S(1)}) all-reduce(f32[1,32]{1,0:T(1,128)S(1)} %get-tuple-element.27, f32[1,32]{1,0:T(1,128)S(1)} %get-tuple-element.26), channel_id=1, replica_groups=mesh['groups'=1,'frames'=32] {'frames'}, use_global_device_ids=true, to_apply=%region_2.3 | all-reduce | flops 64 | bytes 512 | tf_op jit(solution)/shard_map/psum | solution.py:60
  62.4 1.1 multiply_convert_fusion.1
  63.9 2.0 %fusion.17 = f32[256,640]{1,0:T(8,128)S(1)} fusion(bf16[256,640]{1,0:T(8,128)(2,1)S(1)} %bitcast.123, bf16[9,640,640]{2,1,0:T(8,128)(2,1)} %param.14), kind=kOutput, calls=%fused_computation.31 | convolution fusion | flops 209715200 | bytes 1802240 | tf_op jit(solution)/shard_map/dot_general | solution.py:81
  65.8 1.6 %convolution_add_fusion.8 = f32[256,640]{1,0:T(8,128)S(1)} fusion(f32[256,640]{1,0:T(8,128)S(1)} %fusion.17, bf16[256,640]{1,0:T(8,128)(2,1)S(1)} %bitcast.122, bf16[9,640,640]{2,1,0:T(8,128)(2,1)} %param.14), kind=kOutput, calls=%fused_computation.17 | convolution fusion | flops 209879040 | bytes 2457600 | tf_op jit(solution)/shard_map/dot_general | solution.py:81
  67.5 0.5 convolution_add_fusion.7
  67.9 0.5 convolution_add_fusion.6
  68.4 0.5 convolution_add_fusion.5
  69.3 0.5 convolution_add_fusion.3
  69.8 0.5 convolution_add_fusion.2
  70.3 0.6 fusion.39
  71.1 1.0 fusion.1
  72.1 28.5 %all_to_all.12 = bf16[1,32,8,1920]{3,2,0,1:T(8,128)(2,1)} all-to-all(bf16[1,32,8,1920]{3,2,0,1:T(8,128)(2,1)S(1)} %fusion.1), channel_id=1, replica_groups=mesh['groups'=1,'frames'=32] {'frames'}, dimensions={1} | all-to-all | bytes 1966080 | tf_op jit(solution)/shard_map/all_to_all | solution.py:94
  100.6 4.4 %reshape.253 = bf16[1,32,8,3,10,64]{5,4,3,2,1,0:T(8,128)(2,1)} reshape(bf16[1,32,8,1920]{3,2,0,1:T(8,128)(2,1)} %all_to_all.12) | data formatting | bytes 1966080 | tf_op jit(solution)/shard_map/reshape | solution.py:21
  105.0 4.2 %fusion.38 = (bf16[1,32,8,1,10,64]{5,4,3,2,1,0:T(8,128)(2,1)}, bf16[1,32,8,1,10,64]{5,4,3,2,1,0:T(8,128)(2,1)}, bf16[1,32,8,1,10,64]{5,4,3,2,1,0:T(8,128)(2,1)}) fusion(bf16[1,32,8,3,10,64]{5,4,3,2,1,0:T(8,128)(2,1)} %reshape.253), kind=kLoop, calls=%fused_computation.74 | loop fusion | bytes 1966080 | tf_op jit(solution)/shard_map/slice | solution.py:24
  109.2 3.8 %fusion.40 = (f32[8,10,32]{2,1,0:T(8,128)S(1)}, f32[8,10,32,32]{2,3,1,0:T(8,128)}) fusion(bf16[1,32,8,1,10,64]{5,4,3,2,1,0:T(8,128)(2,1)} %get-tuple-element.11, bf16[1,32,8,1,10,64]{5,4,3,2,1,0:T(8,128)(2,1)} %get-tuple-element.10), kind=kOutput, calls=%fused_computation.76 | convolution fusion | flops 10731551 | bytes 993280 | tf_op jit(solution)/shard_map/sub | solution.py:28
  112.9 2.2 %fusion.4 = bf16[1,32,8,10,64]{4,1,3,2,0:T(8,128)(2,1)S(1)} fusion(f32[8,10,32,32]{2,3,1,0:T(8,128)} %get-tuple-element.25, bf16[1,32,8,1,10,64]{5,4,3,2,1,0:T(8,128)(2,1)} %get-tuple-element.9, f32[8,10,32]{2,1,0:T(8,128)S(1)} %get-tuple-element.24), kind=kOutput, calls=%fused_computation.8 | convolution fusion | flops 10813440 | bytes 993280 | tf_op jit(solution)/shard_map/aphts,asphd->atphd/dot_general | solution.py:31
  115.2 1.3 copy.21
  116.5 1.8 %reshape.257 = bf16[32,1,8,640]{3,2,0,1:T(8,128)(2,1)S(1)} reshape(bf16[1,32,8,10,64]{4,3,2,1,0:T(8,128)(2,1)} %copy.21) | data formatting | bytes 655360 | tf_op jit(solution)/shard_map/reshape | solution.py:34
  118.4 15.4 %all_to_all.13 = bf16[32,1,8,640]{3,2,1,0:T(8,128)(2,1)S(1)} all-to-all(bf16[32,1,8,640]{3,2,1,0:T(8,128)(2,1)S(1)} %bitcast.116), channel_id=1, replica_groups=mesh['groups'=1,'frames'=32] {'frames'}, dimensions={0} | all-to-all | bytes 655360 | tf_op jit(solution)/shard_map/all_to_all | solution.py:96
  133.8 2.3 %fusion.8 = bf16[1,256,640]{2,1,0:T(8,128)(2,1)} fusion(f32[256,640]{1,0:T(8,128)S(1)} %get-tuple-element.23, bf16[640,640]{1,0:T(8,128)(2,1)} %param.17, bf16[32,1,8,640]{3,2,1,0:T(8,128)(2,1)S(1)} %all_to_all.13), kind=kOutput, calls=%fused_computation.22 | convolution fusion | flops 210042880 | bytes 2129920 | tf_op jit(solution)/shard_map/dot_general | solution.py:97
  (25 shorter events, 1.8 us)
Async XLA Ops:
  0.0 71.1 %copy-start = (bf16[640,1920]{1,0:T(8,128)(2,1)S(1)}, bf16[640,1920]{1,0:T(8,128)(2,1)}, u32[]{:S(2)}) copy-start(bf16[640,1920]{1,0:T(8,128)(2,1)} %param.16) | copy-start | bytes 7372804
  0.0 62.4 %copy-start.2 = (bf16[1,256,640]{2,1,0:T(8,128)(2,1)S(1)}, bf16[1,256,640]{2,1,0:T(8,128)(2,1)}, u32[]{:S(2)}) copy-start(bf16[1,256,640]{2,1,0:T(8,128)(2,1)} %param.9) | copy-start | bytes 983044
  2.6 19.3 %all-to-all-start = ((bf16[32,8,640]{2,1,0:T(8,128)(2,1)}), bf16[32,8,640]{2,1,0:T(8,128)(2,1)S(1)}, u32[]{:S(2)}, u32[]{:S(2)}) async-start(bf16[32,8,640]{2,1,0:T(8,128)(2,1)} %fusion.7), calls=%async_computation | async-start | bytes 655360 | tf_op jit(solution)/shard_map/all_to_all | solution.py:46
  62.4 5.0 %copy-start.1 = (bf16[9,640,640]{2,1,0:T(8,128)(2,1)S(1)}, bf16[9,640,640]{2,1,0:T(8,128)(2,1)}, u32[]{:S(2)}) copy-start(bf16[9,640,640]{2,1,0:T(8,128)(2,1)} %param.14) | copy-start | bytes 22118404
  68.8 1.4 %copy-start.3 = (bf16[1,256,640]{2,1,0:T(8,128)(2,1)S(1)}, bf16[1,256,640]{2,1,0:T(8,128)(2,1)}, u32[]{:S(2)}) copy-start(bf16[1,256,640]{2,1,0:T(8,128)(2,1)} %param.9) | copy-start | bytes 983044
  69.8 1.3 copy-start.4
where the time goes:
time: 137 us; the launch traced here: 136 us
  blocking collectives  82.5 us (60%)
  matrix products  18.8 us (14%)
  local copies, waits for them, and re-layouts  12.6 us (9%)
  waiting for transfers between devices  12 us (9%)
  starting transfers between devices  7.3 us (5%)
  other arithmetic  2.73 us (2%)
    psum x1, blocking collectives, body(): total_sums, total_sq = lax.psum((clip_sums, clip_sq), 'frames')  38.6 us
    all_to_all x1, blocking collectives, body(): lax.all_to_all(qkv_rows, 'frames', split_axis=1, concat_axis=0, tiled=True)  28.5 us
    all_to_all x1, blocking collectives, body(): lax.all_to_all(attended, 'frames', split_axis=0, concat_axis=1, tiled=True)  15.4 us
    all_to_all x1, waiting for transfers between devices, body(): lax.all_to_all(zero_out, 'frames', split_axis=0, concat_axis=1, tiled=True)  12 us
    all_to_all x1, starting transfers between devices, body(): lax.all_to_all(zero_out, 'frames', split_axis=0, concat_axis=1, tiled=True)  7.3 us
    dot_general x9, matrix products, body(): jnp.dot(window, conv_weight[tap_index], preferred_element_type=jnp.float32)  6.89 us
    reshape x1, local copies, waits for them, and re-layouts, attend_block(): shaped = qkv_rows.reshape(clip_count, CLIP, count, 3, HEADS, HD)  4.38 us
    slice x1, local copies, waits for them, and re-layouts, attend_block(): value_rows = shaped[:, :, :, 2]  4.21 us
  transfers between devices with their start and end apart: 1, of which 1 were waited for; matrix products, arithmetic and copies ran while one was open for 0% of the time, Pallas kernels for 0%

commit v1 on v0

v1 whole, which is shorter than its diff:
```python
import functools
import math

import jax
import jax.numpy as jnp
from jax import lax
from jax.experimental import pallas as pl
from jax.experimental.pallas import tpu as pltpu
from jax.sharding import PartitionSpec as P

HEADS = 10
HD = 64
GROUPS = 32
CLIP = 32
W = 32
LANES = 128
EPS = 1e-05
MESH = pl.DeviceIdType.MESH
HIGH = lax.Precision.HIGHEST
F32 = jnp.float32
BF16 = jnp.bfloat16


def kernel(
    n, fused_entry,
    skip_hbm, entry_hbm, zero_hbm, gain_ref, bias_ref, conv_hbm, ln_ref, qkv_hbm, wout_hbm,
    out_ref,
    skip_ref, entry_ref, zero_ref, conv_ref, qkv_ref, wout_ref,
    zero_send, zero_recv, joined, stat_send, stat_recv, window, norm_send, norm_recv,
    att_send, att_recv, load_sem, send_sem, recv_sem,
):
    me = lax.axis_index("frames")
    rows, chans = skip_ref.shape
    base = me // CLIP * CLIP
    spot = lax.rem(me, CLIP)

    loads = [
        pltpu.make_async_copy(src, dst, load_sem.at[i])
        for i, (src, dst) in enumerate([
            (entry_hbm, entry_ref), (zero_hbm, zero_ref), (skip_hbm, skip_ref),
            (conv_hbm, conv_ref), (qkv_hbm, qkv_ref), (wout_hbm, wout_ref),
        ])
    ]
    for load in loads:
        load.start()

    barrier = pltpu.get_barrier_semaphore()
    first, count, mine = (0, n, me) if fused_entry else (base, CLIP, spot)

    def greet(step, carry):
        pl.semaphore_signal(
            barrier, inc=1, device_id={"frames": first + lax.rem(mine + step, count)},
            device_id_type=MESH,
        )
        return carry

    lax.fori_loop(1, count, greet, 0)

    def exchange(phase, origin, total, place, pick, recv):
        def push(step, carry):
            other = lax.rem(place + step, total)
            pltpu.make_async_remote_copy(
                src_ref=pick(other), dst_ref=recv.at[place],
                send_sem=send_sem.at[phase], recv_sem=recv_sem.at[phase],
                device_id={"frames": origin + other}, device_id_type=MESH,
            ).start()
            return carry

        lax.fori_loop(1, total, push, 0)

    def arrive(phase, total, recv):
        part = recv.at[pl.ds(0, total - 1)]
        pltpu.make_async_copy(part, part, recv_sem.at[phase]).wait()

    def leave(phase, total, recv):
        part = recv.at[pl.ds(0, total - 1)]
        pltpu.make_async_copy(part, part, send_sem.at[phase]).wait()

    def flat(value):
        return value.astype(F32).reshape(-1, value.shape[-1])

    loads[0].wait()
    loads[1].wait()
    if fused_entry:
        zero_out = jnp.dot(entry_ref[...], zero_ref[...], preferred_element_type=F32)
        zero_send[...] = zero_out.reshape(zero_send.shape).astype(BF16)
        zero_recv[me] = zero_send[me]
    pl.semaphore_wait(barrier, count - 1)
    if fused_entry:
        exchange(0, 0, n, me, lambda other: zero_send.at[other], zero_recv)

    width = chans // GROUPS
    members = (
        lax.broadcasted_iota(jnp.int32, (chans, LANES), 0) // width
        == lax.broadcasted_iota(jnp.int32, (chans, LANES), 1)
    ).astype(F32)
    members_t = (
        lax.broadcasted_iota(jnp.int32, (LANES, chans), 1) // width
        == lax.broadcasted_iota(jnp.int32, (LANES, chans), 0)
    ).astype(F32)
    window[:W, :] = jnp.zeros((W, window.shape[1]), BF16)
    window[rows + W:, :] = jnp.zeros((W, window.shape[1]), BF16)
    loads[2].wait()

    if fused_entry:
        arrive(0, n, zero_recv)
        entry = flat(zero_recv[...])
    else:
        entry = entry_ref[...].astype(F32)
    together = skip_ref[...].astype(F32) + entry
    joined[...] = together
    sums = jnp.sum(together, axis=0, keepdims=True)
    squares = jnp.sum(together * together, axis=0, keepdims=True)
    lead = lax.broadcasted_iota(jnp.int32, (8, chans), 0)
    both = jnp.where(lead == 0, sums, jnp.where(lead == 1, squares, 0.0))
    stat_send[...] = jnp.dot(both, members, preferred_element_type=F32, precision=HIGH)
    stat_recv[spot] = stat_send[...]
    exchange(1, base, CLIP, spot, lambda other: stat_send, stat_recv)
    arrive(1, CLIP, stat_recv)
    size = float(CLIP * rows * width)
    totals = jnp.sum(stat_recv[...], axis=0) / size
    group_mean = totals[0:1, :]
    group_var = totals[1:2, :] - group_mean * group_mean
    group_inv = lax.rsqrt(group_var + EPS)
    lead = lax.broadcasted_iota(jnp.int32, (8, LANES), 0)
    both = jnp.where(lead == 0, group_mean, jnp.where(lead == 1, group_inv, 0.0))
    spread = jnp.dot(both, members_t, preferred_element_type=F32, precision=HIGH)
    value = (joined[...] - spread[0:1, :]) * spread[1:2, :] * gain_ref[...] + bias_ref[...]
    active = value / (1.0 + jnp.exp(-value))
    active = active.astype(BF16).astype(F32)

    column = lax.rem(lax.broadcasted_iota(jnp.int32, (rows, chans), 0), W)
    body_rows = slice(W, rows + W)
    window[body_rows, 0:chans] = jnp.where(column == 0, 0.0, pltpu.roll(active, 1, 0)).astype(BF16)
    window[body_rows, chans:2 * chans] = active.astype(BF16)
    window[body_rows, 2 * chans:] = jnp.where(
        column == W - 1, 0.0, pltpu.roll(active, rows - 1, 0)
    ).astype(BF16)
    loads[3].wait()
    resid = joined[...]
    for tap in range(3):
        resid = resid + jnp.dot(
            window[tap * W:tap * W + rows, :], conv_ref[tap], preferred_element_type=F32
        )
    joined[...] = resid

    mean = jnp.mean(resid, axis=-1, keepdims=True)
    centred = resid - mean
    var = jnp.mean(centred * centred, axis=-1, keepdims=True)
    normed = centred * lax.rsqrt(var + EPS) * ln_ref[...]
    norm_send[...] = normed.reshape(norm_send.shape).astype(BF16)
    norm_recv[spot] = norm_send[spot]
    exchange(2, base, CLIP, spot, lambda other: norm_send.at[other], norm_recv)
    loads[4].wait()
    loads[5].wait()
    arrive(2, CLIP, norm_recv)

    pix = norm_send.shape[1]
    tokens = flat(norm_recv[...]).astype(BF16)
    qkv = jnp.dot(tokens, qkv_ref[...], preferred_element_type=F32).astype(BF16)
    same = (
        lax.rem(lax.broadcasted_iota(jnp.int32, (rows, rows), 0), pix)
        == lax.rem(lax.broadcasted_iota(jnp.int32, (rows, rows), 1), pix)
    )
    low = lax.broadcasted_iota(jnp.int32, (rows, LANES), 1) < HD
    scale = 1.0 / math.sqrt(HD)
    for pair in range(chans // LANES):
        lo = pair * LANES
        queries = qkv[:, lo:lo + LANES].astype(F32) * scale
        keys = qkv[:, chans + lo:chans + lo + LANES]
        values = qkv[:, 2 * chans + lo:2 * chans + lo + LANES]
        mixed = []
        for half in (low, jnp.logical_not(low)):
            scores = lax.dot_general(
                jnp.where(half, queries, 0.0).astype(BF16), keys, (((1,), (1,)), ((), ())),
                preferred_element_type=F32,
            )
            scores = jnp.where(same, scores, -jnp.inf)
            expon = jnp.exp(scores - jnp.max(scores, axis=-1, keepdims=True))
            weights = (expon / jnp.sum(expon, axis=-1, keepdims=True)).astype(BF16)
            mixed.append(jnp.dot(weights, values, preferred_element_type=F32))
        result = jnp.where(low, mixed[0], mixed[1])
        att_send[:, :, lo:lo + LANES] = result.reshape(CLIP, pix, LANES).astype(BF16)
    att_recv[spot] = att_send[spot]
    exchange(3, base, CLIP, spot, lambda other: att_send.at[other], att_recv)
    arrive(3, CLIP, att_recv)
    attended = flat(att_recv[...]).astype(BF16)
    out_ref[...] = (
        joined[...] + jnp.dot(attended, wout_ref[...], preferred_element_type=F32)
    ).astype(BF16)
    if fused_entry:
        leave(0, n, zero_recv)
    leave(1, CLIP, stat_recv)
    leave(2, CLIP, norm_recv)
    leave(3, CLIP, att_recv)


def body(
    skip, control, zero_weight, gn_gain, gn_bias, conv_weight, ln_gain, qkv_weight, out_weight
):
    f_dev, rows, chans = skip.shape
    n = lax.axis_size("frames")
    frames, pix_dev, _ = control.shape
    assert f_dev == 1 and n % CLIP == 0 and rows % CLIP == 0
    fused_entry = pix_dev % 8 == 0
    if fused_entry:
        entry = control.reshape(frames * pix_dev, chans)
        entry_block = (n, pix_dev, chans)
    else:
        zero_out = jnp.dot(
            control.reshape(-1, chans), zero_weight, preferred_element_type=F32
        ).astype(BF16).reshape(control.shape)
        entry = lax.all_to_all(
            zero_out, "frames", split_axis=0, concat_axis=1, tiled=True
        ).reshape(rows, chans)
        entry_block = (8, 8, LANES)
    pix = rows // CLIP
    block = (CLIP, pix, chans)
    any_spec = pl.BlockSpec(memory_space=pl.ANY)
    vmem_spec = pl.BlockSpec(memory_space=pltpu.VMEM)
    call = pl.pallas_call(
        functools.partial(kernel, n, fused_entry),
        out_shape=jax.ShapeDtypeStruct((rows, chans), BF16),
        in_specs=[
            any_spec, any_spec, any_spec, vmem_spec, vmem_spec, any_spec, vmem_spec,
            any_spec, any_spec,
        ],
        out_specs=vmem_spec,
        scratch_shapes=[
            pltpu.VMEM((rows, chans), BF16),
            pltpu.VMEM(entry.shape, BF16),
            pltpu.VMEM(zero_weight.shape, BF16),
            pltpu.VMEM((3, 3 * chans, chans), BF16),
            pltpu.VMEM(qkv_weight.shape, BF16),
            pltpu.VMEM(out_weight.shape, BF16),
            pltpu.VMEM(entry_block, BF16),
            pltpu.VMEM(entry_block, BF16),
            pltpu.VMEM((rows, chans), F32),
            pltpu.VMEM((8, LANES), F32),
            pltpu.VMEM((CLIP, 8, LANES), F32),
            pltpu.VMEM((rows + 2 * W, 3 * chans), BF16),
            pltpu.VMEM(block, BF16),
            pltpu.VMEM(block, BF16),
            pltpu.VMEM(block, BF16),
            pltpu.VMEM(block, BF16),
            pltpu.SemaphoreType.DMA((6,)),
            pltpu.SemaphoreType.DMA((4,)),
            pltpu.SemaphoreType.DMA((4,)),
        ],
        compiler_params=pltpu.CompilerParams(
            collective_id=0, has_side_effects=True, vmem_limit_bytes=48 * 1024 * 1024
        ),
    )
    out = call(
        skip.reshape(rows, chans), entry, zero_weight, gn_gain.reshape(1, chans),
        gn_bias.reshape(1, chans), conv_weight.reshape(3, 3 * chans, chans),
        ln_gain.reshape(1, chans), qkv_weight, out_weight,
    )
    return out.reshape(skip.shape)


def solution(mesh):
    frames = P(("groups", "frames"), None, None)
    return jax.shard_map(
        body, mesh=mesh,
        in_specs=(frames, P("groups", "frames", None), P(), P(), P(), P(), P(), P(), P()),
        out_specs=frames, check_vma=False,
    )
```

time: 137 us -> 54.8 us (0.40)
  the two profiles are of different devices: /device:TPU:0 before, /device:TPU:25 now
where the time goes in v1:
time: 54.8 us; the launch traced here: 54.4 us
  Pallas kernels  45.6 us (83%)
  local copies, waits for them, and re-layouts  8.72 us (16%)
    pallas_call x1, Pallas kernels, body(): call(skip.reshape(rows, chans), entry, zero_weight, gn_gain.reshape(1, ch...  45.6 us
    unnamed x11, local copies, waits for them, and re-layouts  6.65 us

profile of v1, /device:TPU:25, one launch (start us, length us, event | category | flops | bytes accessed | tf_op | source)
XLA Modules:
  0.0 54.4 jit_solution(7809189280524148009)
XLA Ops:
  0.0 0.7 %reshape.23.gain_ref = f32[1,640]{1,0:T(1,128)S(1)} reshape(f32[640]{0:T(1024)} %param.12) | data formatting | bytes 5120 | tf_op jit(solution)/shard_map/reshape | solution.py:255
  0.7 0.7 %reshape.24.bias_ref = f32[1,640]{1,0:T(1,128)S(1)} reshape(f32[640]{0:T(1024)} %param.13) | data formatting | bytes 5120 | tf_op jit(solution)/shard_map/reshape | solution.py:256
  1.4 0.7 %reshape.26.ln_ref = f32[1,640]{1,0:T(1,128)S(1)} reshape(f32[640]{0:T(1024)} %param.15) | data formatting | bytes 5120 | tf_op jit(solution)/shard_map/reshape | solution.py:257
  2.1 0.0 copy-start
  2.1 1.7 %copy-done = bf16[640,1920]{1,0:T(8,128)(2,1)S(1)} copy-done((bf16[640,1920]{1,0:T(8,128)(2,1)S(1)}, bf16[640,1920]{1,0:T(8,128)(2,1)}, u32[]{:S(2)}) %copy-start) | copy-done | bytes 2457624
  3.8 0.0 copy-start.1
  3.8 1.1 %copy-done.1 = bf16[640,640]{1,0:T(8,128)(2,1)S(1)} copy-done((bf16[640,640]{1,0:T(8,128)(2,1)S(1)}, bf16[640,640]{1,0:T(8,128)(2,1)}, u32[]{:S(2)}) %copy-start.1) | copy-done | bytes 819224
  4.9 0.0 copy-start.2
  4.9 1.1 %copy-done.2 = bf16[640,640]{1,0:T(8,128)(2,1)S(1)} copy-done((bf16[640,640]{1,0:T(8,128)(2,1)S(1)}, bf16[640,640]{1,0:T(8,128)(2,1)}, u32[]{:S(2)}) %copy-start.2) | copy-done | bytes 819224
  6.1 0.0 copy-start.3
  6.1 1.0 %copy-done.3 = bf16[1,256,640]{2,1,0:T(8,128)(2,1)S(1)} copy-done((bf16[1,256,640]{2,1,0:T(8,128)(2,1)S(1)}, bf16[1,256,640]{2,1,0:T(8,128)(2,1)}, u32[]{:S(2)}) %copy-start.3) | copy-done | bytes 327704
  7.0 0.0 copy-start.4
  7.0 1.0 %copy-done.4 = bf16[32,8,640]{2,1,0:T(8,128)(2,1)S(1)} copy-done((bf16[32,8,640]{2,1,0:T(8,128)(2,1)S(1)}, bf16[32,8,640]{2,1,0:T(8,128)(2,1)}, u32[]{:S(2)}) %copy-start.4) | copy-done | bytes 327704
  8.0 45.6 %shard_map.91 = bf16[256,640]{1,0:T(8,128)(2,1)S(1)} custom-call(bf16[256,640]{1,0:T(8,128)(2,1)S(1)} %bitcast.5, bf16[256,640]{1,0:T(8,128)(2,1)S(1)} %bitcast.6, bf16[640,640]{1,0:T(8,128)(2,1)S(1)} %copy-done.1, f32[1,640]{1,0:T(1,128)S(1)} %reshape.23.gain_ref, f32[1,640]{1,0:T(1,128)S(1)} %reshape.24.bias_ref, bf16[3,1920,640]{2,1,0:T(8,128)(2,1)} %bitcast.7, ...), custom_call_target="tpu_custom_call" | custom-call | tf_op jit(solution)/shard_map/pallas_call | solution.py:254
  53.7 0.7 %copy.11 = bf16[1,256,640]{2,1,0:T(8,128)(2,1)} copy(bf16[1,256,640]{2,1,0:T(8,128)(2,1)S(1)} %bitcast.4) | data formatting | bytes 655360
Async XLA Ops:
  2.1 1.7 %copy-start = (bf16[640,1920]{1,0:T(8,128)(2,1)S(1)}, bf16[640,1920]{1,0:T(8,128)(2,1)}, u32[]{:S(2)}) copy-start(bf16[640,1920]{1,0:T(8,128)(2,1)} %qkv_hbm.1) | copy-start | bytes 7372804
  3.8 1.1 %copy-start.1 = (bf16[640,640]{1,0:T(8,128)(2,1)S(1)}, bf16[640,640]{1,0:T(8,128)(2,1)}, u32[]{:S(2)}) copy-start(bf16[640,640]{1,0:T(8,128)(2,1)} %zero_hbm.1) | copy-start | bytes 2457604
  4.9 1.1 %copy-start.2 = (bf16[640,640]{1,0:T(8,128)(2,1)S(1)}, bf16[640,640]{1,0:T(8,128)(2,1)}, u32[]{:S(2)}) copy-start(bf16[640,640]{1,0:T(8,128)(2,1)} %wout_hbm.1) | copy-start | bytes 2457604
  6.1 1.0 %copy-start.3 = (bf16[1,256,640]{2,1,0:T(8,128)(2,1)S(1)}, bf16[1,256,640]{2,1,0:T(8,128)(2,1)}, u32[]{:S(2)}) copy-start(bf16[1,256,640]{2,1,0:T(8,128)(2,1)} %param.9) | copy-start | bytes 983044
  7.0 1.0 %copy-start.4 = (bf16[32,8,640]{2,1,0:T(8,128)(2,1)S(1)}, bf16[32,8,640]{2,1,0:T(8,128)(2,1)}, u32[]{:S(2)}) copy-start(bf16[32,8,640]{2,1,0:T(8,128)(2,1)} %param.10) | copy-start | bytes 983044

commit v2 on v1

--- a/solution.py
+++ b/solution.py
@@ -16,16 +16,34 @@
 LANES = 128
 EPS = 1e-05
 MESH = pl.DeviceIdType.MESH
-HIGH = lax.Precision.HIGHEST
 F32 = jnp.float32
 BF16 = jnp.bfloat16
 
 
+def parts(row):
+    top = row.astype(BF16).astype(F32)
+    middle = (row - top).astype(BF16).astype(F32)
+    return [top, middle, row - top - middle]
+
+
+def pool(first, second, matrix):
+    rows = parts(first) + parts(second)
+    lead = lax.broadcasted_iota(jnp.int32, (16, first.shape[1]), 0)
+    stack = jnp.zeros(lead.shape, F32)
+    for i, row in enumerate(rows):
+        stack = jnp.where(lead == i, row, stack)
+    product = jnp.dot(stack.astype(BF16), matrix, preferred_element_type=F32)
+    return (
+        product[0:1] + product[1:2] + product[2:3],
+        product[3:4] + product[4:5] + product[5:6],
+    )
+
+
 def kernel(
     n, fused_entry,
-    skip_hbm, entry_hbm, zero_hbm, gain_ref, bias_ref, conv_hbm, ln_ref, qkv_hbm, wout_hbm,
+    skip_hbm, entry_hbm, zero_hbm, gain_hbm, bias_hbm, conv_hbm, ln_hbm, qkv_hbm, wout_hbm,
     out_ref,
-    skip_ref, entry_ref, zero_ref, conv_ref, qkv_ref, wout_ref,
+    skip_ref, entry_ref, zero_ref, conv_ref, qkv_ref, wout_ref, gain_ref, bias_ref, ln_ref,
     zero_send, zero_recv, joined, stat_send, stat_recv, window, norm_send, norm_recv,
     att_send, att_recv, load_sem, send_sem, recv_sem,
 ):
@@ -39,6 +57,7 @@
         for i, (src, dst) in enumerate([
             (entry_hbm, entry_ref), (zero_hbm, zero_ref), (skip_hbm, skip_ref),
             (conv_hbm, conv_ref), (qkv_hbm, qkv_ref), (wout_hbm, wout_ref),
+            (gain_hbm, gain_ref), (bias_hbm, bias_ref), (ln_hbm, ln_ref),
         ])
     ]
     for load in loads:
@@ -92,12 +111,12 @@
     width = chans // GROUPS
     members = (
         lax.broadcasted_iota(jnp.int32, (chans, LANES), 0) // width
-        == lax.broadcasted_iota(jnp.int32, (chans, LANES), 1)
-    ).astype(F32)
+        == lax.rem(lax.broadcasted_iota(jnp.int32, (chans, LANES), 1), GROUPS)
+    ).astype(F32).astype(BF16)
     members_t = (
         lax.broadcasted_iota(jnp.int32, (LANES, chans), 1) // width
-        == lax.broadcasted_iota(jnp.int32, (LANES, chans), 0)
-    ).astype(F32)
+        == lax.rem(lax.broadcasted_iota(jnp.int32, (LANES, chans), 0), GROUPS)
+    ).astype(F32).astype(BF16)
     window[:W, :] = jnp.zeros((W, window.shape[1]), BF16)
     window[rows + W:, :] = jnp.zeros((W, window.shape[1]), BF16)
     loads[2].wait()
@@ -111,21 +130,25 @@
     joined[...] = together
     sums = jnp.sum(together, axis=0, keepdims=True)
     squares = jnp.sum(together * together, axis=0, keepdims=True)
-    lead = lax.broadcasted_iota(jnp.int32, (8, chans), 0)
-    both = jnp.where(lead == 0, sums, jnp.where(lead == 1, squares, 0.0))
-    stat_send[...] = jnp.dot(both, members, preferred_element_type=F32, precision=HIGH)
+    sums, squares = pool(sums, squares, members)
+    lane = lax.broadcasted_iota(jnp.int32, (1, LANES), 1)
+    stat_send[...] = jnp.where(lane < GROUPS, sums, squares)
     stat_recv[spot] = stat_send[...]
     exchange(1, base, CLIP, spot, lambda other: stat_send, stat_recv)
     arrive(1, CLIP, stat_recv)
     size = float(CLIP * rows * width)
     totals = jnp.sum(stat_recv[...], axis=0) / size
-    group_mean = totals[0:1, :]
-    group_var = totals[1:2, :] - group_mean * group_mean
-    group_inv = lax.rsqrt(group_var + EPS)
-    lead = lax.broadcasted_iota(jnp.int32, (8, LANES), 0)
-    both = jnp.where(lead == 0, group_mean, jnp.where(lead == 1, group_inv, 0.0))
-    spread = jnp.dot(both, members_t, preferred_element_type=F32, precision=HIGH)
-    value = (joined[...] - spread[0:1, :]) * spread[1:2, :] * gain_ref[...] + bias_ref[...]
+    group_mean, group_sq = pool(
+        jnp.where(lane < GROUPS, totals, 0.0),
+        jnp.where((lane >= GROUPS) & (lane < 2 * GROUPS), totals, 0.0),
+        members_t,
+    )
+    group_inv = lax.rsqrt(group_sq - group_mean * group_mean + EPS)
+    loads[6].wait()
+    loads[7].wait()
+    gain = gain_ref[...].reshape(1, chans)
+    bias = bias_ref[...].reshape(1, chans)
+    value = (joined[...] - group_mean) * group_inv * gain + bias
     active = value / (1.0 + jnp.exp(-value))
     active = active.astype(BF16).astype(F32)
 
@@ -144,10 +167,11 @@
         )
     joined[...] = resid
 
+    loads[8].wait()
     mean = jnp.mean(resid, axis=-1, keepdims=True)
     centred = resid - mean
     var = jnp.mean(centred * centred, axis=-1, keepdims=True)
-    normed = centred * lax.rsqrt(var + EPS) * ln_ref[...]
+    normed = centred * lax.rsqrt(var + EPS) * ln_ref[...].reshape(1, chans)
     norm_send[...] = normed.reshape(norm_send.shape).astype(BF16)
     norm_recv[spot] = norm_send[spot]
     exchange(2, base, CLIP, spot, lambda other: norm_send.at[other], norm_recv)
@@ -177,7 +201,7 @@
             )
             scores = jnp.where(same, scores, -jnp.inf)
             expon = jnp.exp(scores - jnp.max(scores, axis=-1, keepdims=True))
-            weights = (expon / jnp.sum(expon, axis=-1, keepdims=True)).astype(BF16)
+            weights = (expon * (1.0 / jnp.sum(expon, axis=-1, keepdims=True))).astype(BF16)
             mixed.append(jnp.dot(weights, values, preferred_element_type=F32))
         result = jnp.where(low, mixed[0], mixed[1])
         att_send[:, :, lo:lo + LANES] = result.reshape(CLIP, pix, LANES).astype(BF16)
@@ -216,15 +240,12 @@
         entry_block = (8, 8, LANES)
     pix = rows // CLIP
     block = (CLIP, pix, chans)
-    any_spec = pl.BlockSpec(memory_space=pl.ANY)
+    hbm_spec = pl.BlockSpec(memory_space=pltpu.HBM)
     vmem_spec = pl.BlockSpec(memory_space=pltpu.VMEM)
     call = pl.pallas_call(
         functools.partial(kernel, n, fused_entry),
         out_shape=jax.ShapeDtypeStruct((rows, chans), BF16),
-        in_specs=[
-            any_spec, any_spec, any_spec, vmem_spec, vmem_spec, any_spec, vmem_spec,
-            any_spec, any_spec,
-        ],
+        in_specs=[hbm_spec] * 9,
         out_specs=vmem_spec,
         scratch_shapes=[
             pltpu.VMEM((rows, chans), BF16),
@@ -233,28 +254,30 @@
             pltpu.VMEM((3, 3 * chans, chans), BF16),
             pltpu.VMEM(qkv_weight.shape, BF16),
             pltpu.VMEM(out_weight.shape, BF16),
+            pltpu.VMEM((chans,), F32),
+            pltpu.VMEM((chans,), F32),
+            pltpu.VMEM((chans,), F32),
             pltpu.VMEM(entry_block, BF16),
             pltpu.VMEM(entry_block, BF16),
             pltpu.VMEM((rows, chans), F32),
-            pltpu.VMEM((8, LANES), F32),
-            pltpu.VMEM((CLIP, 8, LANES), F32),
+            pltpu.VMEM((1, LANES), F32),
+            pltpu.VMEM((CLIP, 1, LANES), F32),
             pltpu.VMEM((rows + 2 * W, 3 * chans), BF16),
             pltpu.VMEM(block, BF16),
             pltpu.VMEM(block, BF16),
             pltpu.VMEM(block, BF16),
             pltpu.VMEM(block, BF16),
-            pltpu.SemaphoreType.DMA((6,)),
+            pltpu.SemaphoreType.DMA((9,)),
             pltpu.SemaphoreType.DMA((4,)),
             pltpu.SemaphoreType.DMA((4,)),
         ],
         compiler_params=pltpu.CompilerParams(
-            collective_id=0, has_side_effects=True, vmem_limit_bytes=48 * 1024 * 1024
+            collective_id=0, has_side_effects=True, vmem_limit_bytes=60 * 1024 * 1024
         ),
     )
     out = call(
-        skip.reshape(rows, chans), entry, zero_weight, gn_gain.reshape(1, chans),
-        gn_bias.reshape(1, chans), conv_weight.reshape(3, 3 * chans, chans),
-        ln_gain.reshape(1, chans), qkv_weight, out_weight,
+        skip.reshape(rows, chans), entry, zero_weight, gn_gain, gn_bias,
+        conv_weight.reshape(3, 3 * chans, chans), ln_gain, qkv_weight, out_weight,
     )
     return out.reshape(skip.shape)
 

time: 54.8 us -> 45.8 us (0.84)
  local copies, waits for them, and re-layouts: 8.72 us -> 1.73 us
  Pallas kernels: 45.6 us -> 44 us
    unnamed x11 -> x1, local copies, waits for them, and re-layouts: 6.65 us -> 1.73 us
    reshape x3 -> x0, local copies, waits for them, and re-layouts: 2.07 us -> none  [the longest x1 0.69 us: body(): gn_gain.reshape(1, chans)]
    pallas_call x1, Pallas kernels: 45.6 us -> 44 us  [body(): call(skip.reshape(rows, chans), entry, zero_weight, gn_gain, gn_bias, con...]
where the time goes in v2:
time: 45.8 us; the launch traced here: 45.7 us
  Pallas kernels  44 us (96%)
  local copies, waits for them, and re-layouts  1.73 us (4%)
    pallas_call x1, Pallas kernels, body(): call(skip.reshape(rows, chans), entry, zero_weight, gn_gain, gn_bias, con...  44 us
    unnamed x1, local copies, waits for them, and re-layouts  1.73 us

profile of v2, /device:TPU:25, one launch (start us, length us, event | category | flops | bytes accessed | tf_op | source)
XLA Modules:
  0.0 45.7 jit_solution(9394815416487768022)
XLA Ops:
  0.0 44.0 %shard_map.91 = bf16[256,640]{1,0:T(8,128)(2,1)} custom-call(bf16[256,640]{1,0:T(8,128)(2,1)} %bitcast.6, bf16[256,640]{1,0:T(8,128)(2,1)} %bitcast.7, bf16[640,640]{1,0:T(8,128)(2,1)} %zero_hbm.1, f32[640]{0:T(1024)} %gain_hbm.1, f32[640]{0:T(1024)} %bias_hbm.1, bf16[3,1920,640]{2,1,0:T(8,128)(2,1)} %bitcast.4, f32[640]{0:T(1024)} %ln_hbm.1, ...), custom_call_target="tpu_custom_call" | custom-call | tf_op jit(solution)/shard_map/pallas_call | solution.py:278
  44.0 1.7 %copy.11 = bf16[1,256,640]{2,1,0:T(8,128)(2,1)} copy(bf16[1,256,640]{2,1,0:T(8,128)(2,1)} %bitcast.5) | data formatting | bytes 655360

commit v3 on v2

--- a/solution.py
+++ b/solution.py
@@ -14,6 +14,7 @@
 CLIP = 32
 W = 32
 LANES = 128
+HALVES = 2
 EPS = 1e-05
 MESH = pl.DeviceIdType.MESH
 F32 = jnp.float32
@@ -51,6 +52,8 @@
     rows, chans = skip_ref.shape
     base = me // CLIP * CLIP
     spot = lax.rem(me, CLIP)
+    per = CLIP // HALVES
+    own_block = lax.rem(spot, HALVES) * per + spot // HALVES
 
     loads = [
         pltpu.make_async_copy(src, dst, load_sem.at[i])
@@ -60,7 +63,7 @@
             (gain_hbm, gain_ref), (bias_hbm, bias_ref), (ln_hbm, ln_ref),
         ])
     ]
-    for load in loads:
+    for load in loads[:3]:
         load.start()
 
     barrier = pltpu.get_barrier_semaphore()
@@ -75,11 +78,11 @@
 
     lax.fori_loop(1, count, greet, 0)
 
-    def exchange(phase, origin, total, place, pick, recv):
+    def exchange(phase, origin, total, place, pick, recv, slot):
         def push(step, carry):
             other = lax.rem(place + step, total)
             pltpu.make_async_remote_copy(
-                src_ref=pick(other), dst_ref=recv.at[place],
+                src_ref=pick(other), dst_ref=recv.at[slot],
                 send_sem=send_sem.at[phase], recv_sem=recv_sem.at[phase],
                 device_id={"frames": origin + other}, device_id_type=MESH,
             ).start()
@@ -100,13 +103,15 @@
 
     loads[0].wait()
     loads[1].wait()
+    for load in loads[3:]:
+        load.start()
     if fused_entry:
         zero_out = jnp.dot(entry_ref[...], zero_ref[...], preferred_element_type=F32)
         zero_send[...] = zero_out.reshape(zero_send.shape).astype(BF16)
         zero_recv[me] = zero_send[me]
     pl.semaphore_wait(barrier, count - 1)
     if fused_entry:
-        exchange(0, 0, n, me, lambda other: zero_send.at[other], zero_recv)
+        exchange(0, 0, n, me, lambda other: zero_send.at[other], zero_recv, me)
 
     width = chans // GROUPS
     members = (
@@ -134,7 +139,7 @@
     lane = lax.broadcasted_iota(jnp.int32, (1, LANES), 1)
     stat_send[...] = jnp.where(lane < GROUPS, sums, squares)
     stat_recv[spot] = stat_send[...]
-    exchange(1, base, CLIP, spot, lambda other: stat_send, stat_recv)
+    exchange(1, base, CLIP, spot, lambda other: stat_send, stat_recv, spot)
     arrive(1, CLIP, stat_recv)
     size = float(CLIP * rows * width)
     totals = jnp.sum(stat_recv[...], axis=0) / size
@@ -160,21 +165,42 @@
         column == W - 1, 0.0, pltpu.roll(active, rows - 1, 0)
     ).astype(BF16)
     loads[3].wait()
-    resid = joined[...]
-    for tap in range(3):
-        resid = resid + jnp.dot(
-            window[tap * W:tap * W + rows, :], conv_ref[tap], preferred_element_type=F32
-        )
-    joined[...] = resid
-
     loads[8].wait()
-    mean = jnp.mean(resid, axis=-1, keepdims=True)
-    centred = resid - mean
-    var = jnp.mean(centred * centred, axis=-1, keepdims=True)
-    normed = centred * lax.rsqrt(var + EPS) * ln_ref[...].reshape(1, chans)
-    norm_send[...] = normed.reshape(norm_send.shape).astype(BF16)
-    norm_recv[spot] = norm_send[spot]
-    exchange(2, base, CLIP, spot, lambda other: norm_send.at[other], norm_recv)
+    ln_gain = ln_ref[...].reshape(1, chans)
+    deep = rows // HALVES
+    for half in range(HALVES):
+        top = half * deep
+        resid = joined[top:top + deep, :]
+        for tap in range(3):
+            start = top + tap * W
+            resid = resid + jnp.dot(
+                window[start:start + deep, :], conv_ref[tap], preferred_element_type=F32
+            )
+        joined[top:top + deep, :] = resid
+        mean = jnp.mean(resid, axis=-1, keepdims=True)
+        centred = resid - mean
+        var = jnp.mean(centred * centred, axis=-1, keepdims=True)
+        normed = centred * lax.rsqrt(var + EPS) * ln_gain
+        norm_send[half * per:(half + 1) * per] = normed.reshape(
+            (per,) + norm_send.shape[1:]
+        ).astype(BF16)
+
+        def push(step, carry, half=half):
+            place = lax.rem(step + spot // HALVES, per)
+            other = place * HALVES + half
+
+            @pl.when(other != spot)
+            def _():
+                pltpu.make_async_remote_copy(
+                    src_ref=norm_send.at[half * per + place], dst_ref=norm_recv.at[spot],
+                    send_sem=send_sem.at[2], recv_sem=recv_sem.at[2],
+                    device_id={"frames": base + other}, device_id_type=MESH,
+                ).start()
+
+            return carry
+
+        lax.fori_loop(1, per + 1, push, 0)
+    norm_recv[spot] = norm_send[own_block]
     loads[4].wait()
     loads[5].wait()
     arrive(2, CLIP, norm_recv)
@@ -205,8 +231,8 @@
             mixed.append(jnp.dot(weights, values, preferred_element_type=F32))
         result = jnp.where(low, mixed[0], mixed[1])
         att_send[:, :, lo:lo + LANES] = result.reshape(CLIP, pix, LANES).astype(BF16)
-    att_recv[spot] = att_send[spot]
-    exchange(3, base, CLIP, spot, lambda other: att_send.at[other], att_recv)
+    att_recv[own_block] = att_send[spot]
+    exchange(3, base, CLIP, spot, lambda other: att_send.at[other], att_recv, own_block)
     arrive(3, CLIP, att_recv)
     attended = flat(att_recv[...]).astype(BF16)
     out_ref[...] = (

time: 45.8 us -> 43.4 us (0.948)
  the two profiles are of different devices: /device:TPU:25 before, /device:TPU:0 now
where the time goes in v3:
time: 43.4 us; the launch traced here: 42.7 us
  Pallas kernels  41 us (94%)
  local copies, waits for them, and re-layouts  1.73 us (4%)
    pallas_call x1, Pallas kernels, body(): call(skip.reshape(rows, chans), entry, zero_weight, gn_gain, gn_bias, con...  41 us
    unnamed x1, local copies, waits for them, and re-layouts  1.73 us

profile of v3, /device:TPU:0, one launch (start us, length us, event | category | flops | bytes accessed | tf_op | source)
XLA Modules:
  0.0 42.7 jit_solution(15212332550617906662)
XLA Ops:
  0.0 41.0 %shard_map.91 = bf16[256,640]{1,0:T(8,128)(2,1)} custom-call(bf16[256,640]{1,0:T(8,128)(2,1)} %bitcast.6, bf16[256,640]{1,0:T(8,128)(2,1)} %bitcast.7, bf16[640,640]{1,0:T(8,128)(2,1)} %zero_hbm.1, f32[640]{0:T(1024)} %gain_hbm.1, f32[640]{0:T(1024)} %bias_hbm.1, bf16[3,1920,640]{2,1,0:T(8,128)(2,1)} %bitcast.4, f32[640]{0:T(1024)} %ln_hbm.1, ...), custom_call_target="tpu_custom_call" | custom-call | tf_op jit(solution)/shard_map/pallas_call | solution.py:304
  41.0 1.7 %copy.11 = bf16[1,256,640]{2,1,0:T(8,128)(2,1)} copy(bf16[1,256,640]{2,1,0:T(8,128)(2,1)} %bitcast.5) | data formatting | bytes 655360

commit v4 on v3

--- a/solution.py
+++ b/solution.py
@@ -46,7 +46,7 @@
     out_ref,
     skip_ref, entry_ref, zero_ref, conv_ref, qkv_ref, wout_ref, gain_ref, bias_ref, ln_ref,
     zero_send, zero_recv, joined, stat_send, stat_recv, window, norm_send, norm_recv,
-    att_send, att_recv, load_sem, send_sem, recv_sem,
+    att_send_a, att_send_b, att_recv_a, att_recv_b, load_sem, send_sem, recv_sem,
 ):
     me = lax.axis_index("frames")
     rows, chans = skip_ref.shape
@@ -81,14 +81,18 @@
     def exchange(phase, origin, total, place, pick, recv, slot):
         def push(step, carry):
             other = lax.rem(place + step, total)
-            pltpu.make_async_remote_copy(
-                src_ref=pick(other), dst_ref=recv.at[slot],
-                send_sem=send_sem.at[phase], recv_sem=recv_sem.at[phase],
-                device_id={"frames": origin + other}, device_id_type=MESH,
-            ).start()
+
+            @pl.when(other != place)
+            def _():
+                pltpu.make_async_remote_copy(
+                    src_ref=pick(other), dst_ref=recv.at[slot],
+                    send_sem=send_sem.at[phase], recv_sem=recv_sem.at[phase],
+                    device_id={"frames": origin + other}, device_id_type=MESH,
+                ).start()
+
             return carry
 
-        lax.fori_loop(1, total, push, 0)
+        lax.fori_loop(total // 4, total + total // 4, push, 0)
 
     def arrive(phase, total, recv):
         part = recv.at[pl.ds(0, total - 1)]
@@ -97,6 +101,10 @@
     def leave(phase, total, recv):
         part = recv.at[pl.ds(0, total - 1)]
         pltpu.make_async_copy(part, part, send_sem.at[phase]).wait()
+
+    def give_back(phase, source, recv):
+        recv[own_block] = source[spot]
+        exchange(phase, base, CLIP, spot, lambda other: source.at[other], recv, own_block)
 
     def flat(value):
         return value.astype(F32).reshape(-1, value.shape[-1])
@@ -199,7 +207,7 @@
 
             return carry
 
-        lax.fori_loop(1, per + 1, push, 0)
+        lax.fori_loop(per // 4, per + per // 4, push, 0)
     norm_recv[spot] = norm_send[own_block]
     loads[4].wait()
     loads[5].wait()
@@ -214,8 +222,10 @@
     )
     low = lax.broadcasted_iota(jnp.int32, (rows, LANES), 1) < HD
     scale = 1.0 / math.sqrt(HD)
+    split = att_send_a.shape[-1]
     for pair in range(chans // LANES):
         lo = pair * LANES
+        att_send, col = (att_send_a, lo) if lo < split else (att_send_b, lo - split)
         queries = qkv[:, lo:lo + LANES].astype(F32) * scale
         keys = qkv[:, chans + lo:chans + lo + LANES]
         values = qkv[:, 2 * chans + lo:2 * chans + lo + LANES]
@@ -230,19 +240,26 @@
             weights = (expon * (1.0 / jnp.sum(expon, axis=-1, keepdims=True))).astype(BF16)
             mixed.append(jnp.dot(weights, values, preferred_element_type=F32))
         result = jnp.where(low, mixed[0], mixed[1])
-        att_send[:, :, lo:lo + LANES] = result.reshape(CLIP, pix, LANES).astype(BF16)
-    att_recv[own_block] = att_send[spot]
-    exchange(3, base, CLIP, spot, lambda other: att_send.at[other], att_recv, own_block)
-    arrive(3, CLIP, att_recv)
-    attended = flat(att_recv[...]).astype(BF16)
+        att_send[:, :, col:col + LANES] = result.reshape(CLIP, pix, LANES).astype(BF16)
+        if lo + LANES == split:
+            give_back(3, att_send_a, att_recv_a)
+    give_back(4, att_send_b, att_recv_b)
+    arrive(3, CLIP, att_recv_a)
+    partial = joined[...] + jnp.dot(
+        flat(att_recv_a[...]).astype(BF16), wout_ref[:split, :], preferred_element_type=F32
+    )
+    arrive(4, CLIP, att_recv_b)
     out_ref[...] = (
-        joined[...] + jnp.dot(attended, wout_ref[...], preferred_element_type=F32)
+        partial + jnp.dot(
+            flat(att_recv_b[...]).astype(BF16), wout_ref[split:, :], preferred_element_type=F32
+        )
     ).astype(BF16)
     if fused_entry:
         leave(0, n, zero_recv)
     leave(1, CLIP, stat_recv)
     leave(2, CLIP, norm_recv)
-    leave(3, CLIP, att_recv)
+    leave(3, CLIP, att_recv_a)
+    leave(4, CLIP, att_recv_b)
 
 
 def body(
@@ -266,6 +283,7 @@
         entry_block = (8, 8, LANES)
     pix = rows // CLIP
     block = (CLIP, pix, chans)
+    early = (chans // LANES + 1) // 2 * LANES
     hbm_spec = pl.BlockSpec(memory_space=pltpu.HBM)
     vmem_spec = pl.BlockSpec(memory_space=pltpu.VMEM)
     call = pl.pallas_call(
@@ -291,11 +309,13 @@
             pltpu.VMEM((rows + 2 * W, 3 * chans), BF16),
             pltpu.VMEM(block, BF16),
             pltpu.VMEM(block, BF16),
-            pltpu.VMEM(block, BF16),
-            pltpu.VMEM(block, BF16),
+            pltpu.VMEM(block[:2] + (early,), BF16),
+            pltpu.VMEM(block[:2] + (chans - early,), BF16),
+            pltpu.VMEM(block[:2] + (early,), BF16),
+            pltpu.VMEM(block[:2] + (chans - early,), BF16),
             pltpu.SemaphoreType.DMA((9,)),
-            pltpu.SemaphoreType.DMA((4,)),
-            pltpu.SemaphoreType.DMA((4,)),
+            pltpu.SemaphoreType.DMA((5,)),
+            pltpu.SemaphoreType.DMA((5,)),
         ],
         compiler_params=pltpu.CompilerParams(
             collective_id=0, has_side_effects=True, vmem_limit_bytes=60 * 1024 * 1024

time: 43.4 us -> 45.1 us (1.039); the launches traced: 42.7 us -> 45 us
  Pallas kernels: 41 us -> 43.2 us
    pallas_call x1, Pallas kernels: 41 us -> 43.2 us  [body(): call(skip.reshape(rows, chans), entry, zero_weight, gn_gain, gn_bias, con...]
where the time goes in v4:
time: 45.1 us; the launch traced here: 45 us
  Pallas kernels  43.2 us (96%)
  local copies, waits for them, and re-layouts  1.73 us (4%)
    pallas_call x1, Pallas kernels, body(): call(skip.reshape(rows, chans), entry, zero_weight, gn_gain, gn_bias, con...  43.2 us
    unnamed x1, local copies, waits for them, and re-layouts  1.73 us

profile of v4, /device:TPU:0, one launch (start us, length us, event | category | flops | bytes accessed | tf_op | source)
XLA Modules:
  0.0 45.0 jit_solution(16752203614781555283)
XLA Ops:
  0.0 43.2 %shard_map.91 = bf16[256,640]{1,0:T(8,128)(2,1)} custom-call(bf16[256,640]{1,0:T(8,128)(2,1)} %bitcast.6, bf16[256,640]{1,0:T(8,128)(2,1)} %bitcast.7, bf16[640,640]{1,0:T(8,128)(2,1)} %zero_hbm.1, f32[640]{0:T(1024)} %gain_hbm.1, f32[640]{0:T(1024)} %bias_hbm.1, bf16[3,1920,640]{2,1,0:T(8,128)(2,1)} %bitcast.4, f32[640]{0:T(1024)} %ln_hbm.1, ...), custom_call_target="tpu_custom_call" | custom-call | tf_op jit(solution)/shard_map/pallas_call | solution.py:324
  43.2 1.7 %copy.11 = bf16[1,256,640]{2,1,0:T(8,128)(2,1)} copy(bf16[1,256,640]{2,1,0:T(8,128)(2,1)} %bitcast.5) | data formatting | bytes 655360

commit v5 on v3

--- a/solution.py
+++ b/solution.py
@@ -69,26 +69,20 @@
     barrier = pltpu.get_barrier_semaphore()
     first, count, mine = (0, n, me) if fused_entry else (base, CLIP, spot)
 
-    def greet(step, carry):
+    for step in range(1, count):
         pl.semaphore_signal(
             barrier, inc=1, device_id={"frames": first + lax.rem(mine + step, count)},
             device_id_type=MESH,
         )
-        return carry
-
-    lax.fori_loop(1, count, greet, 0)
 
     def exchange(phase, origin, total, place, pick, recv, slot):
-        def push(step, carry):
+        for step in range(1, total):
             other = lax.rem(place + step, total)
             pltpu.make_async_remote_copy(
                 src_ref=pick(other), dst_ref=recv.at[slot],
                 send_sem=send_sem.at[phase], recv_sem=recv_sem.at[phase],
                 device_id={"frames": origin + other}, device_id_type=MESH,
             ).start()
-            return carry
-
-        lax.fori_loop(1, total, push, 0)
 
     def arrive(phase, total, recv):
         part = recv.at[pl.ds(0, total - 1)]
@@ -97,6 +91,13 @@
     def leave(phase, total, recv):
         part = recv.at[pl.ds(0, total - 1)]
         pltpu.make_async_copy(part, part, send_sem.at[phase]).wait()
+
+    def give_row(block, other):
+        pltpu.make_async_remote_copy(
+            src_ref=norm_send.at[block], dst_ref=norm_recv.at[spot],
+            send_sem=send_sem.at[2], recv_sem=recv_sem.at[2],
+            device_id={"frames": base + other}, device_id_type=MESH,
+        ).start()
 
     def flat(value):
         return value.astype(F32).reshape(-1, value.shape[-1])
@@ -185,21 +186,13 @@
             (per,) + norm_send.shape[1:]
         ).astype(BF16)
 
-        def push(step, carry, half=half):
-            place = lax.rem(step + spot // HALVES, per)
-            other = place * HALVES + half
-
-            @pl.when(other != spot)
-            def _():
-                pltpu.make_async_remote_copy(
-                    src_ref=norm_send.at[half * per + place], dst_ref=norm_recv.at[spot],
-                    send_sem=send_sem.at[2], recv_sem=recv_sem.at[2],
-                    device_id={"frames": base + other}, device_id_type=MESH,
-                ).start()
-
-            return carry
-
-        lax.fori_loop(1, per + 1, push, 0)
+        for step in range(1, per):
+            place = lax.rem(spot // HALVES + step, per)
+            give_row(half * per + place, place * HALVES + half)
+    for step in range(1, HALVES):
+        half = lax.rem(spot + step, HALVES)
+        place = spot // HALVES
+        give_row(half * per + place, place * HALVES + half)
     norm_recv[spot] = norm_send[own_block]
     loads[4].wait()
     loads[5].wait()

time: 43.4 us -> 43.2 us (level)
  no operation moved by 1% of the time
where the time goes in v5:
time: 43.2 us; the launch traced here: 42.7 us
  Pallas kernels  40.9 us (95%)
  local copies, waits for them, and re-layouts  1.73 us (4%)
    pallas_call x1, Pallas kernels, body(): call(skip.reshape(rows, chans), entry, zero_weight, gn_gain, gn_bias, con...  40.9 us
    unnamed x1, local copies, waits for them, and re-layouts  1.73 us

profile of v5, /device:TPU:0, one launch (start us, length us, event | category | flops | bytes accessed | tf_op | source)
XLA Modules:
  0.0 42.7 jit_solution(8776384235049870418)
XLA Ops:
  0.0 40.9 %shard_map.91 = bf16[256,640]{1,0:T(8,128)(2,1)} custom-call(bf16[256,640]{1,0:T(8,128)(2,1)} %bitcast.6, bf16[256,640]{1,0:T(8,128)(2,1)} %bitcast.7, bf16[640,640]{1,0:T(8,128)(2,1)} %zero_hbm.1, f32[640]{0:T(1024)} %gain_hbm.1, f32[640]{0:T(1024)} %bias_hbm.1, bf16[3,1920,640]{2,1,0:T(8,128)(2,1)} %bitcast.4, f32[640]{0:T(1024)} %ln_hbm.1, ...), custom_call_target="tpu_custom_call" | custom-call | tf_op jit(solution)/shard_map/pallas_call | solution.py:297
  40.9 1.7 %copy.11 = bf16[1,256,640]{2,1,0:T(8,128)(2,1)} copy(bf16[1,256,640]{2,1,0:T(8,128)(2,1)} %bitcast.5) | data formatting | bytes 655360

commit v6 on v5

--- a/solution.py
+++ b/solution.py
@@ -15,6 +15,7 @@
 W = 32
 LANES = 128
 HALVES = 2
+PIXEL_SETS = 2
 EPS = 1e-05
 MESH = pl.DeviceIdType.MESH
 F32 = jnp.float32
@@ -46,7 +47,7 @@
     out_ref,
     skip_ref, entry_ref, zero_ref, conv_ref, qkv_ref, wout_ref, gain_ref, bias_ref, ln_ref,
     zero_send, zero_recv, joined, stat_send, stat_recv, window, norm_send, norm_recv,
-    att_send, att_recv, load_sem, send_sem, recv_sem,
+    att_send, att_recv, att_sorted, load_sem, send_sem, recv_sem,
 ):
     me = lax.axis_index("frames")
     rows, chans = skip_ref.shape
@@ -194,36 +195,54 @@
         place = spot // HALVES
         give_row(half * per + place, place * HALVES + half)
     norm_recv[spot] = norm_send[own_block]
+    pix = norm_send.shape[1]
+    few = pix // PIXEL_SETS
+    block = CLIP * few
+
+    def source(sorted_row):
+        within = lax.rem(sorted_row, block)
+        return within // few * pix + sorted_row // block * few + lax.rem(within, few)
+
+    across = lax.broadcasted_iota(jnp.int32, (rows, rows), 0)
+    along = lax.broadcasted_iota(jnp.int32, (rows, rows), 1)
+    order = (source(across) == along).astype(F32).astype(BF16)
+    order_back = (source(along) == across).astype(F32).astype(BF16)
     loads[4].wait()
     loads[5].wait()
     arrive(2, CLIP, norm_recv)
 
-    pix = norm_send.shape[1]
-    tokens = flat(norm_recv[...]).astype(BF16)
+    tokens = jnp.dot(
+        order, flat(norm_recv[...]).astype(BF16), preferred_element_type=F32
+    ).astype(BF16)
     qkv = jnp.dot(tokens, qkv_ref[...], preferred_element_type=F32).astype(BF16)
     same = (
-        lax.rem(lax.broadcasted_iota(jnp.int32, (rows, rows), 0), pix)
-        == lax.rem(lax.broadcasted_iota(jnp.int32, (rows, rows), 1), pix)
-    )
-    low = lax.broadcasted_iota(jnp.int32, (rows, LANES), 1) < HD
+        lax.rem(lax.broadcasted_iota(jnp.int32, (block, block), 0), few)
+        == lax.rem(lax.broadcasted_iota(jnp.int32, (block, block), 1), few)
+    )
+    low = lax.broadcasted_iota(jnp.int32, (block, LANES), 1) < HD
     scale = 1.0 / math.sqrt(HD)
     for pair in range(chans // LANES):
         lo = pair * LANES
-        queries = qkv[:, lo:lo + LANES].astype(F32) * scale
-        keys = qkv[:, chans + lo:chans + lo + LANES]
-        values = qkv[:, 2 * chans + lo:2 * chans + lo + LANES]
-        mixed = []
-        for half in (low, jnp.logical_not(low)):
-            scores = lax.dot_general(
-                jnp.where(half, queries, 0.0).astype(BF16), keys, (((1,), (1,)), ((), ())),
-                preferred_element_type=F32,
-            )
-            scores = jnp.where(same, scores, -jnp.inf)
-            expon = jnp.exp(scores - jnp.max(scores, axis=-1, keepdims=True))
-            weights = (expon * (1.0 / jnp.sum(expon, axis=-1, keepdims=True))).astype(BF16)
-            mixed.append(jnp.dot(weights, values, preferred_element_type=F32))
-        result = jnp.where(low, mixed[0], mixed[1])
-        att_send[:, :, lo:lo + LANES] = result.reshape(CLIP, pix, LANES).astype(BF16)
+        for top in range(0, rows, block):
+            queries = qkv[top:top + block, lo:lo + LANES].astype(F32) * scale
+            keys = qkv[top:top + block, chans + lo:chans + lo + LANES]
+            values = qkv[top:top + block, 2 * chans + lo:2 * chans + lo + LANES]
+            mixed = []
+            for half in (low, jnp.logical_not(low)):
+                scores = lax.dot_general(
+                    jnp.where(half, queries, 0.0).astype(BF16), keys, (((1,), (1,)), ((), ())),
+                    preferred_element_type=F32,
+                )
+                scores = jnp.where(same, scores, -jnp.inf)
+                expon = jnp.exp(scores - jnp.max(scores, axis=-1, keepdims=True))
+                weights = (expon * (1.0 / jnp.sum(expon, axis=-1, keepdims=True))).astype(BF16)
+                mixed.append(jnp.dot(weights, values, preferred_element_type=F32))
+            att_sorted[top:top + block, lo:lo + LANES] = jnp.where(
+                low, mixed[0], mixed[1]
+            ).astype(BF16)
+    att_send[...] = jnp.dot(
+        order_back, att_sorted[...], preferred_element_type=F32
+    ).reshape(att_send.shape).astype(BF16)
     att_recv[own_block] = att_send[spot]
     exchange(3, base, CLIP, spot, lambda other: att_send.at[other], att_recv, own_block)
     arrive(3, CLIP, att_recv)
@@ -286,6 +305,7 @@
             pltpu.VMEM(block, BF16),
             pltpu.VMEM(block, BF16),
             pltpu.VMEM(block, BF16),
+            pltpu.VMEM((rows, chans), BF16),
             pltpu.SemaphoreType.DMA((9,)),
             pltpu.SemaphoreType.DMA((4,)),
             pltpu.SemaphoreType.DMA((4,)),

time: 43.2 us -> 47.9 us (1.11)
  Pallas kernels: 40.9 us -> 45.6 us
    pallas_call x1, Pallas kernels: 40.9 us -> 45.6 us  [body(): call(skip.reshape(rows, chans), entry, zero_weight, gn_gain, gn_bias, con...]
where the time goes in v6:
time: 47.9 us; the launch traced here: 47.3 us
  Pallas kernels  45.6 us (95%)
  local copies, waits for them, and re-layouts  1.73 us (4%)
    pallas_call x1, Pallas kernels, body(): call(skip.reshape(rows, chans), entry, zero_weight, gn_gain, gn_bias, con...  45.6 us
    unnamed x1, local copies, waits for them, and re-layouts  1.73 us

profile of v6, /device:TPU:0, one launch (start us, length us, event | category | flops | bytes accessed | tf_op | source)
XLA Modules:
  0.0 47.3 jit_solution(17750363204137852966)
XLA Ops:
  0.0 45.6 %shard_map.91 = bf16[256,640]{1,0:T(8,128)(2,1)} custom-call(bf16[256,640]{1,0:T(8,128)(2,1)} %bitcast.6, bf16[256,640]{1,0:T(8,128)(2,1)} %bitcast.7, bf16[640,640]{1,0:T(8,128)(2,1)} %zero_hbm.1, f32[640]{0:T(1024)} %gain_hbm.1, f32[640]{0:T(1024)} %bias_hbm.1, bf16[3,1920,640]{2,1,0:T(8,128)(2,1)} %bitcast.4, f32[640]{0:T(1024)} %ln_hbm.1, ...), custom_call_target="tpu_custom_call" | custom-call | tf_op jit(solution)/shard_map/pallas_call | solution.py:317
  45.6 1.7 %copy.11 = bf16[1,256,640]{2,1,0:T(8,128)(2,1)} copy(bf16[1,256,640]{2,1,0:T(8,128)(2,1)} %bitcast.5) | data formatting | bytes 655360

commit v7 on v5

--- a/solution.py
+++ b/solution.py
@@ -46,7 +46,7 @@
     out_ref,
     skip_ref, entry_ref, zero_ref, conv_ref, qkv_ref, wout_ref, gain_ref, bias_ref, ln_ref,
     zero_send, zero_recv, joined, stat_send, stat_recv, window, norm_send, norm_recv,
-    att_send, att_recv, load_sem, send_sem, recv_sem,
+    att_send, att_recv, scores, weights, load_sem, send_sem, recv_sem,
 ):
     me = lax.axis_index("frames")
     rows, chans = skip_ref.shape
@@ -207,21 +207,28 @@
     )
     low = lax.broadcasted_iota(jnp.int32, (rows, LANES), 1) < HD
     scale = 1.0 / math.sqrt(HD)
-    for pair in range(chans // LANES):
+    halves = (low, jnp.logical_not(low))
+    pairs = chans // LANES
+    for pair in range(pairs):
         lo = pair * LANES
         queries = qkv[:, lo:lo + LANES].astype(F32) * scale
         keys = qkv[:, chans + lo:chans + lo + LANES]
-        values = qkv[:, 2 * chans + lo:2 * chans + lo + LANES]
-        mixed = []
-        for half in (low, jnp.logical_not(low)):
-            scores = lax.dot_general(
+        for side, half in enumerate(halves):
+            scores[2 * pair + side] = lax.dot_general(
                 jnp.where(half, queries, 0.0).astype(BF16), keys, (((1,), (1,)), ((), ())),
                 preferred_element_type=F32,
             )
-            scores = jnp.where(same, scores, -jnp.inf)
-            expon = jnp.exp(scores - jnp.max(scores, axis=-1, keepdims=True))
-            weights = (expon * (1.0 / jnp.sum(expon, axis=-1, keepdims=True))).astype(BF16)
-            mixed.append(jnp.dot(weights, values, preferred_element_type=F32))
+    for head in range(2 * pairs):
+        masked = jnp.where(same, scores[head], -jnp.inf)
+        expon = jnp.exp(masked - jnp.max(masked, axis=-1, keepdims=True))
+        weights[head] = (expon * (1.0 / jnp.sum(expon, axis=-1, keepdims=True))).astype(BF16)
+    for pair in range(pairs):
+        lo = pair * LANES
+        values = qkv[:, 2 * chans + lo:2 * chans + lo + LANES]
+        mixed = [
+            jnp.dot(weights[2 * pair + side], values, preferred_element_type=F32)
+            for side in range(2)
+        ]
         result = jnp.where(low, mixed[0], mixed[1])
         att_send[:, :, lo:lo + LANES] = result.reshape(CLIP, pix, LANES).astype(BF16)
     att_recv[own_block] = att_send[spot]
@@ -286,6 +293,8 @@
             pltpu.VMEM(block, BF16),
             pltpu.VMEM(block, BF16),
             pltpu.VMEM(block, BF16),
+            pltpu.VMEM((HEADS, rows, rows), F32),
+            pltpu.VMEM((HEADS, rows, rows), BF16),
             pltpu.SemaphoreType.DMA((9,)),
             pltpu.SemaphoreType.DMA((4,)),
             pltpu.SemaphoreType.DMA((4,)),

time: 43.2 us -> 42.9 us (level)
  no operation moved by 1% of the time
where the time goes in v7:
time: 42.9 us; the launch traced here: 42.3 us
  Pallas kernels  40.6 us (95%)
  local copies, waits for them, and re-layouts  1.73 us (4%)
    pallas_call x1, Pallas kernels, body(): call(skip.reshape(rows, chans), entry, zero_weight, gn_gain, gn_bias, con...  40.6 us
    unnamed x1, local copies, waits for them, and re-layouts  1.73 us

profile of v7, /device:TPU:0, one launch (start us, length us, event | category | flops | bytes accessed | tf_op | source)
XLA Modules:
  0.0 42.3 jit_solution(12655583864437227800)
XLA Ops:
  0.0 40.6 %shard_map.91 = bf16[256,640]{1,0:T(8,128)(2,1)} custom-call(bf16[256,640]{1,0:T(8,128)(2,1)} %bitcast.6, bf16[256,640]{1,0:T(8,128)(2,1)} %bitcast.7, bf16[640,640]{1,0:T(8,128)(2,1)} %zero_hbm.1, f32[640]{0:T(1024)} %gain_hbm.1, f32[640]{0:T(1024)} %bias_hbm.1, bf16[3,1920,640]{2,1,0:T(8,128)(2,1)} %bitcast.4, f32[640]{0:T(1024)} %ln_hbm.1, ...), custom_call_target="tpu_custom_call" | custom-call | tf_op jit(solution)/shard_map/pallas_call | solution.py:306
  40.6 1.7 %copy.11 = bf16[1,256,640]{2,1,0:T(8,128)(2,1)} copy(bf16[1,256,640]{2,1,0:T(8,128)(2,1)} %bitcast.5) | data formatting | bytes 655360

commit v8 on v7

--- a/solution.py
+++ b/solution.py
@@ -19,6 +19,10 @@
 MESH = pl.DeviceIdType.MESH
 F32 = jnp.float32
 BF16 = jnp.bfloat16
+
+
+def far_first(total):
+    return [*range(total // 4, total), *range(1, total // 4)]
 
 
 def parts(row):
@@ -76,7 +80,7 @@
         )
 
     def exchange(phase, origin, total, place, pick, recv, slot):
-        for step in range(1, total):
+        for step in far_first(total):
             other = lax.rem(place + step, total)
             pltpu.make_async_remote_copy(
                 src_ref=pick(other), dst_ref=recv.at[slot],
@@ -186,7 +190,7 @@
             (per,) + norm_send.shape[1:]
         ).astype(BF16)
 
-        for step in range(1, per):
+        for step in far_first(per):
             place = lax.rem(spot // HALVES + step, per)
             give_row(half * per + place, place * HALVES + half)
     for step in range(1, HALVES):

time: 42.9 us -> 45 us (1.049)
  Pallas kernels: 40.6 us -> 43.1 us
    pallas_call x1, Pallas kernels: 40.6 us -> 43.1 us  [body(): call(skip.reshape(rows, chans), entry, zero_weight, gn_gain, gn_bias, con...]
where the time goes in v8:
time: 45 us; the launch traced here: 44.8 us
  Pallas kernels  43.1 us (96%)
  local copies, waits for them, and re-layouts  1.73 us (4%)
    pallas_call x1, Pallas kernels, body(): call(skip.reshape(rows, chans), entry, zero_weight, gn_gain, gn_bias, con...  43.1 us
    unnamed x1, local copies, waits for them, and re-layouts  1.73 us

profile of v8, /device:TPU:0, one launch (start us, length us, event | category | flops | bytes accessed | tf_op | source)
XLA Modules:
  0.0 44.8 jit_solution(14562230242528829619)
XLA Ops:
  0.0 43.1 %shard_map.91 = bf16[256,640]{1,0:T(8,128)(2,1)} custom-call(bf16[256,640]{1,0:T(8,128)(2,1)} %bitcast.6, bf16[256,640]{1,0:T(8,128)(2,1)} %bitcast.7, bf16[640,640]{1,0:T(8,128)(2,1)} %zero_hbm.1, f32[640]{0:T(1024)} %gain_hbm.1, f32[640]{0:T(1024)} %bias_hbm.1, bf16[3,1920,640]{2,1,0:T(8,128)(2,1)} %bitcast.4, f32[640]{0:T(1024)} %ln_hbm.1, ...), custom_call_target="tpu_custom_call" | custom-call | tf_op jit(solution)/shard_map/pallas_call | solution.py:310
  43.1 1.7 %copy.11 = bf16[1,256,640]{2,1,0:T(8,128)(2,1)} copy(bf16[1,256,640]{2,1,0:T(8,128)(2,1)} %bitcast.5) | data formatting | bytes 655360

commit v9 on v7

--- a/solution.py
+++ b/solution.py
@@ -19,6 +19,10 @@
 MESH = pl.DeviceIdType.MESH
 F32 = jnp.float32
 BF16 = jnp.bfloat16
+
+
+def both_ways(total):
+    return sorted(range(1, total), key=lambda step: min(step, total - step))
 
 
 def parts(row):
@@ -76,7 +80,7 @@
         )
 
     def exchange(phase, origin, total, place, pick, recv, slot):
-        for step in range(1, total):
+        for step in both_ways(total):
             other = lax.rem(place + step, total)
             pltpu.make_async_remote_copy(
                 src_ref=pick(other), dst_ref=recv.at[slot],
@@ -186,7 +190,7 @@
             (per,) + norm_send.shape[1:]
         ).astype(BF16)
 
-        for step in range(1, per):
+        for step in both_ways(per):
             place = lax.rem(spot // HALVES + step, per)
             give_row(half * per + place, place * HALVES + half)
     for step in range(1, HALVES):

time: 42.9 us -> 43.8 us (1.021)
  Pallas kernels: 40.6 us -> 41.2 us
    pallas_call x1, Pallas kernels: 40.6 us -> 41.2 us  [body(): call(skip.reshape(rows, chans), entry, zero_weight, gn_gain, gn_bias, con...]
where the time goes in v9:
time: 43.8 us; the launch traced here: 43 us
  Pallas kernels  41.2 us (94%)
  local copies, waits for them, and re-layouts  1.73 us (4%)
    pallas_call x1, Pallas kernels, body(): call(skip.reshape(rows, chans), entry, zero_weight, gn_gain, gn_bias, con...  41.2 us
    unnamed x1, local copies, waits for them, and re-layouts  1.73 us

profile of v9, /device:TPU:0, one launch (start us, length us, event | category | flops | bytes accessed | tf_op | source)
XLA Modules:
  0.0 43.0 jit_solution(248314650083222155)
XLA Ops:
  0.0 41.2 %shard_map.91 = bf16[256,640]{1,0:T(8,128)(2,1)} custom-call(bf16[256,640]{1,0:T(8,128)(2,1)} %bitcast.6, bf16[256,640]{1,0:T(8,128)(2,1)} %bitcast.7, bf16[640,640]{1,0:T(8,128)(2,1)} %zero_hbm.1, f32[640]{0:T(1024)} %gain_hbm.1, f32[640]{0:T(1024)} %bias_hbm.1, bf16[3,1920,640]{2,1,0:T(8,128)(2,1)} %bitcast.4, f32[640]{0:T(1024)} %ln_hbm.1, ...), custom_call_target="tpu_custom_call" | custom-call | tf_op jit(solution)/shard_map/pallas_call | solution.py:310
  41.2 1.7 %copy.11 = bf16[1,256,640]{2,1,0:T(8,128)(2,1)} copy(bf16[1,256,640]{2,1,0:T(8,128)(2,1)} %bitcast.5) | data formatting | bytes 655360
